TPU v7x, 32 devices: a whole 2x2x4 slice. The times are simulated.
32 devices in a mesh: segment: 2 (over core), expert: 16 (over z, y, x).
Axes of the slice: x: 2, y: 2, z: 4, core: 2. Of those that a mesh axis runs over, the one named last changes fastest.
Arguments:
- tokens: bfloat16 [2, 1024, 2048], P(None, 'expert'), may hold values from -6 to 6
- routing: int32 [2, 2, 1024, 8], P(None, None, 'expert'), may hold values from 0 to 15, all different within a row; in each aligned block of 64 rows (0 to 63, 64 to 127, ..., all dimensions but the last counted through in order) at most 64 rows name the same one
- norm_gain: bfloat16 [2, 2048], P('segment'), may hold values from 0.5 to 1.5
- router_weight: bfloat16 [2, 2048, 16], P('segment'), may hold values from -0.125 to 0.125
- expert_gate_up: bfloat16 [2, 16, 2048, 768], P('segment', 'expert'), may hold values from -0.125 to 0.125
- expert_down: bfloat16 [2, 16, 384, 2048], P('segment', 'expert'), may hold values from -0.3125 to 0.3125
- pair_index: int32 [64], replicated, may hold values from 0 to 63, each once
- topic_ids: int32 [64], replicated, may hold values from 0 to 7
Outputs:
- final_hidden: bfloat16 [2, 1024, 2048], P('segment', 'expert')
- query_loss: float32 [64], P(('segment', 'expert'))
Inputs may be any that keep to these rules, and one draw needn't show every extreme that they name: `routing`: each row names 8 different experts. In the rows of one device (each aligned block of 64 token rows of one layer and micro-batch) no expert is named by more than 64 rows, a bound that some block reaches. `pair_index`: every passage is the positive of exactly one query.
All inputs are finite; a program needn't handle non-finite values.
Results may differ from a plain program's by a relative error of at most 0.0059.
Values may be sent and summed in bfloat16 or wider, within the bound.
A program may use at most 128 MiB of HBM per device.

v0:
```python
import jax
import jax.numpy as jnp
from jax import lax
from jax.sharding import PartitionSpec as P

SEQ = 16
EPSILON = 1e-06
SOFTMAX_WARMTH = 0.05


def passed_along(block, axis, distance):
    devices = range(lax.axis_size(axis))
    route = [(i - distance, i) for i in devices if i - distance in devices]
    return lax.ppermute(block, axis, route)


def expert_block(received, gate_up, down_proj):
    source_count, slot_count, model_width = received.shape
    flat_rows = received.reshape(source_count * slot_count, model_width)
    projected = jnp.dot(flat_rows, gate_up, preferred_element_type=jnp.float32)
    half_width = gate_up.shape[1] // 2
    hidden = (jax.nn.silu(projected[:, :half_width]) * projected[:, half_width:]).astype(
        jnp.bfloat16
    )
    result = jnp.dot(hidden, down_proj, preferred_element_type=jnp.float32).astype(jnp.bfloat16)
    return result.reshape(source_count, slot_count, model_width)


def moe_layer(inputs, routes, norm_gain, router_weight, gate_up, down_proj):
    row_count, model_width = inputs.shape
    top_count = routes.shape[1]
    expert_count = router_weight.shape[1]
    capacity = 2 * row_count * top_count // expert_count
    widened = inputs.astype(jnp.float32)
    normed = (
        widened
        * lax.rsqrt(jnp.mean(widened * widened, axis=1, keepdims=True) + EPSILON)
        * norm_gain.astype(jnp.float32)
    ).astype(jnp.bfloat16)
    similarity_logits = jnp.dot(normed, router_weight, preferred_element_type=jnp.float32)
    chosen = jnp.take_along_axis(similarity_logits, routes, axis=1)
    raised = jnp.exp(chosen)
    gate_weights = raised / jnp.sum(raised, axis=1, keepdims=True)
    flat_ids = routes.reshape(-1)
    one_hot = (flat_ids[:, None] == jnp.arange(expert_count, dtype=jnp.int32)[None, :]).astype(
        jnp.int32
    )
    earlier = jnp.cumsum(one_hot, axis=0) - one_hot
    slot_index = jnp.sum(earlier * one_hot, axis=1)
    target = flat_ids * capacity + slot_index
    repeated = jnp.repeat(normed, top_count, axis=0)
    outgoing = (
        jnp.zeros((expert_count * capacity, model_width), jnp.bfloat16).at[target].set(repeated)
    )
    outgoing = outgoing.reshape(expert_count, capacity, model_width)
    answered = expert_block(
        lax.all_to_all(outgoing, "expert", split_axis=0, concat_axis=0, tiled=True),
        gate_up,
        down_proj,
    )
    returned = lax.all_to_all(answered, "expert", split_axis=0, concat_axis=0, tiled=True)
    picked = returned.reshape(expert_count * capacity, model_width)[target].astype(jnp.float32)
    picked = picked.reshape(row_count, top_count, model_width)
    mixture = jnp.sum(picked * gate_weights[:, :, None], axis=1)
    return (widened + mixture).astype(jnp.bfloat16)


def pooled_embeddings(final_rows):
    widened = final_rows.astype(jnp.float32)
    pooled = jnp.mean(widened.reshape(-1, SEQ, widened.shape[1]), axis=1)
    return (pooled * lax.rsqrt(jnp.sum(pooled * pooled, axis=1, keepdims=True) + EPSILON)).astype(
        jnp.bfloat16
    )


def local(
    tokens, routing, norm_gain, router_weight, expert_gate_up, expert_down, pair_index, topic_ids
):
    segment_index = lax.axis_index("segment")
    micro_count = tokens.shape[0]
    segment_routes = lax.dynamic_index_in_dim(routing, segment_index, 0, keepdims=False)
    carried = jnp.zeros_like(tokens[0])
    finished = []
    for time_step in range(micro_count + 1):
        fresh_rows = tokens[min(time_step, micro_count - 1)]
        segment_input = jnp.where(segment_index == 0, fresh_rows, carried)
        micro_pick = jnp.clip(time_step - segment_index, 0, micro_count - 1)
        layer_routes = lax.dynamic_index_in_dim(segment_routes, micro_pick, 0, keepdims=False)
        produced = moe_layer(
            segment_input,
            layer_routes,
            norm_gain[0],
            router_weight[0],
            expert_gate_up[0, 0],
            expert_down[0, 0],
        )
        finished.append(produced)
        if time_step < micro_count:
            carried = passed_along(produced, "segment", 1)
    sent_back = passed_along(finished[1], "segment", -1)
    final_rows = jnp.where(segment_index == 0, sent_back, finished[micro_count])
    embedded = pooled_embeddings(final_rows)
    half_count = embedded.shape[0] // 2
    query_vectors = embedded[:half_count]
    passage_vectors = embedded[half_count:]
    device_flat = lax.axis_index(("segment", "expert"))
    columns = jnp.arange(topic_ids.shape[0], dtype=jnp.int32)
    matched = pair_index[:, None] == columns[None, :]
    positive_topic = jnp.sum(
        jnp.where(matched, topic_ids[None, :], jnp.zeros_like(topic_ids)[None, :]), axis=1
    )
    every_query_row = lax.all_gather(query_vectors, ("segment", "expert"), axis=0, tiled=True)
    local_ids = device_flat * half_count + jnp.arange(half_count, dtype=jnp.int32)
    local_topics = lax.dynamic_slice_in_dim(topic_ids, device_flat * half_count, half_count)
    pair_scores = (
        jnp.dot(every_query_row, passage_vectors.T, preferred_element_type=jnp.float32)
        / SOFTMAX_WARMTH
    )
    is_positive = pair_index[:, None] == local_ids[None, :]
    kept_pairs = is_positive | (local_topics[None, :] != positive_topic[:, None])
    partition_part = jnp.sum(
        jnp.where(kept_pairs, jnp.exp(pair_scores), jnp.zeros_like(pair_scores)), axis=1
    )
    positive_part = jnp.sum(
        jnp.where(is_positive, pair_scores, jnp.zeros_like(pair_scores)), axis=1
    )
    partition, positive = (
        lax.psum_scatter(partition_part, ("segment", "expert"), scatter_dimension=0, tiled=True),
        lax.psum_scatter(positive_part, ("segment", "expert"), scatter_dimension=0, tiled=True),
    )
    query_loss = jnp.log(partition) - positive
    return (final_rows[None], query_loss)


def solution(mesh):
    in_specs = (
        P(None, "expert", None),
        P(None, None, "expert", None),
        P("segment", None),
        P("segment", None, None),
        P("segment", "expert", None, None),
        P("segment", "expert", None, None),
        P(),
        P(),
    )
    out_specs = (P("segment", "expert", None), P(("segment", "expert")))
    return jax.shard_map(local, mesh=mesh, in_specs=in_specs, out_specs=out_specs, check_vma=False)
```

profile of v0, /device:TPU:14, one launch (start us, length us, event | category | flops | bytes accessed | tf_op | source)
XLA Modules:
  0.0 794.9 jit_solution(5908741902070264360)
XLA Ops:
  0.7 0.9 bitcast_or_fusion
  1.8 1.2 reduce-window.20
  3.0 0.2 slice_reduce_fusion.2
  3.3 0.1 mul.182
  3.4 1.1 fusion.36
  4.6 0.7 mul.228
  5.4 1.1 fusion.38
  6.5 6.2 scatter_custom_fusion
  12.6 98.8 %all_to_all.30 = bf16[16,64,2048]{2,1,0:T(8,128)(2,1)S(1)} all-to-all(bf16[16,64,2048]{2,1,0:T(8,128)(2,1)} %bitcast.211), channel_id=1, replica_groups=mesh['segment'=2,'expert'=16] {'expert'}, dimensions={0} | all-to-all | bytes 8388608 | tf_op jit(solution)/shard_map/all_to_all | solution.py:57
  111.5 3.4 fusion.7
  114.9 4.3 convolution_convert_fusion.2
  119.2 7.0 all-to-all-start.1
  126.7 1.2 fusion.52
  127.9 3.9 gather_fusion.3
  132.1 1.2 reduce-window.24
  133.2 0.2 slice_reduce_fusion.1
  133.5 84.3 %all-to-all-done.1 = bf16[16,64,2048]{2,1,0:T(8,128)(2,1)} async-done(((bf16[16,64,2048]{2,1,0:T(8,128)(2,1)}), bf16[16,64,2048]{2,1,0:T(8,128)(2,1)}, u32[]{:S(2)}, u32[]{:S(2)}) %all-to-all-start.1) | async-done | bytes 4194336 | tf_op jit(solution)/shard_map/all_to_all | solution.py:61
  217.8 8.0 %gather_fusion = bf16[512,2048]{1,0:T(8,128)(2,1)} fusion(bf16[1024,2048]{1,0:T(8,128)(2,1)} %bitcast.12, s32[1024]{0:T(1024)S(1)} %pad_clamp_fusion.2), kind=kCustom, calls=%fused_computation.3 | custom fusion | bytes 4196352 | tf_op jit(solution)/shard_map/gather | solution.py:62
  225.8 3.4 fusion.2
  229.2 1.7 fusion.39
  230.9 1.3 collective-permute-start
  232.4 0.1 mul.200
  232.5 1.1 collective-permute-done
  233.6 1.1 fusion.42
  234.7 0.7 copy-done.1
  235.4 0.1 fusion.44
  235.6 6.2 scatter_custom_fusion.1
  241.7 97.5 %all_to_all.31 = bf16[16,64,2048]{2,1,0:T(8,128)(2,1)S(1)} all-to-all(bf16[16,64,2048]{2,1,0:T(8,128)(2,1)} %bitcast.213), channel_id=1, replica_groups=mesh['segment'=2,'expert'=16] {'expert'}, dimensions={0} | all-to-all | bytes 8388608 | tf_op jit(solution)/shard_map/all_to_all | solution.py:57
  339.3 3.4 fusion.5
  342.7 4.3 convolution_convert_fusion.1
  347.1 6.3 all-to-all-start.3
  353.8 0.6 fusion.72
  354.4 2.2 reduce-window.26
  356.7 0.2 slice_reduce_fusion
  356.9 0.2 fusion.58
  357.1 3.9 gather_fusion.4
  361.2 0.7 copy.86
  361.9 83.8 %all-to-all-done.3 = bf16[16,64,2048]{2,1,0:T(8,128)(2,1)} async-done(((bf16[16,64,2048]{2,1,0:T(8,128)(2,1)}), bf16[16,64,2048]{2,1,0:T(8,128)(2,1)}, u32[]{:S(2)}, u32[]{:S(2)}) %all-to-all-start.3) | async-done | bytes 4194336 | tf_op jit(solution)/shard_map/all_to_all | solution.py:61
  445.7 8.0 %gather_fusion.1 = bf16[512,2048]{1,0:T(8,128)(2,1)} fusion(bf16[1024,2048]{1,0:T(8,128)(2,1)} %bitcast.25, s32[1024]{0:T(1024)S(1)} %pad_clamp_fusion.1), kind=kCustom, calls=%fused_computation.4 | custom fusion | bytes 4196352 | tf_op jit(solution)/shard_map/gather | solution.py:62
  453.7 3.4 fusion.1
  457.2 0.8 fusion.45
  457.9 2.4 collective-permute-start.2
  460.6 0.1 collective-permute-done.2
  460.7 1.1 fusion.46
  461.9 0.8 fusion.48
  462.7 6.6 scatter_custom_fusion.2
  469.3 97.4 %all_to_all.32 = bf16[16,64,2048]{2,1,0:T(8,128)(2,1)S(1)} all-to-all(bf16[16,64,2048]{2,1,0:T(8,128)(2,1)} %bitcast.212), channel_id=1, replica_groups=mesh['segment'=2,'expert'=16] {'expert'}, dimensions={0} | all-to-all | bytes 8388608 | tf_op jit(solution)/shard_map/all_to_all | solution.py:57
  566.7 3.4 fusion.3
  570.1 4.3 convolution_convert_fusion
  574.5 6.3 all-to-all-start.5
  581.1 0.2 select_reduce_fusion
  581.3 1.5 collective-permute-start.1
  582.7 1.1 fusion.56
  583.9 3.9 gather_fusion.5
  588.1 85.2 %all-to-all-done.5 = bf16[16,64,2048]{2,1,0:T(8,128)(2,1)} async-done(((bf16[16,64,2048]{2,1,0:T(8,128)(2,1)}), bf16[16,64,2048]{2,1,0:T(8,128)(2,1)}, u32[]{:S(2)}, u32[]{:S(2)}) %all-to-all-start.5) | async-done | bytes 4194336 | tf_op jit(solution)/shard_map/all_to_all | solution.py:61
  673.3 8.0 %gather_fusion.2 = bf16[512,2048]{1,0:T(8,128)(2,1)} fusion(bf16[1024,2048]{1,0:T(8,128)(2,1)} %bitcast.36, s32[1024]{0:T(1024)S(1)} %pad_clamp_fusion), kind=kCustom, calls=%fused_computation.5 | custom fusion | bytes 4196352 | tf_op jit(solution)/shard_map/gather | solution.py:62
  681.3 3.4 fusion
  684.8 1.8 convert_reduce_fusion
  686.5 0.1 multiply_reduce_fusion
  686.8 57.1 %all-gather = bf16[32,2,2048]{2,1,0:T(2,128)(2,1)S(1)} all-gather(bf16[1,2,2048]{2,1,0:T(2,128)(2,1)S(1)} %slice_bitcast_fusion), channel_id=1, replica_groups=mesh['segment'=2,'expert'=16] {'segment','expert'}, dimensions={0}, use_global_device_ids=true | all-gather | bytes 270336 | tf_op jit(solution)/shard_map/all_gather | solution.py:112
  743.9 0.8 reshape.399
  744.7 1.1 fusion.76
  745.8 48.3 %all-reduce.2 = (f32[64]{0:T(128)S(1)}, f32[64]{0:T(128)S(1)}) all-reduce(f32[64]{0:T(128)S(1)} %get-tuple-element.4, f32[64]{0:T(128)S(1)} %get-tuple-element.3), channel_id=3, replica_groups=mesh['segment'=2,'expert'=16] {'segment','expert'}, use_global_device_ids=true, to_apply=%region_27.29.clone | all-reduce | flops 128 | bytes 1024
  794.1 0.6 dynamic-slice_subtract_fusion
  (81 shorter events, 3.1 us)
Async XLA Ops:
  0.6 110.8 %copy-start = (bf16[1,1,2048,768]{3,2,1,0:T(8,128)(2,1)S(1)}, bf16[1,1,2048,768]{3,2,1,0:T(8,128)(2,1)}, u32[]{:S(2)}) copy-start(bf16[1,1,2048,768]{3,2,1,0:T(8,128)(2,1)} %param.14) | copy-start | bytes 9437188
  111.5 3.4 copy-start.5
  119.2 7.4 copy-start.3
  119.2 98.5 %all-to-all-start.1 = ((bf16[16,64,2048]{2,1,0:T(8,128)(2,1)}), bf16[16,64,2048]{2,1,0:T(8,128)(2,1)}, u32[]{:S(2)}, u32[]{:S(2)}) async-start(bf16[16,64,2048]{2,1,0:T(8,128)(2,1)} %bitcast.215), calls=%async_computation.1 | async-start | bytes 8388608 | tf_op jit(solution)/shard_map/all_to_all | solution.py:61
  230.9 2.6 collective-permute-start
  234.7 0.7 copy-start.1
  339.3 3.4 copy-start.6
  347.1 98.6 %all-to-all-start.3 = ((bf16[16,64,2048]{2,1,0:T(8,128)(2,1)}), bf16[16,64,2048]{2,1,0:T(8,128)(2,1)}, u32[]{:S(2)}, u32[]{:S(2)}) async-start(bf16[16,64,2048]{2,1,0:T(8,128)(2,1)} %bitcast.216), calls=%async_computation.3 | async-start | bytes 8388608 | tf_op jit(solution)/shard_map/all_to_all | solution.py:61
  356.9 4.1 copy-start.4
  445.7 11.5 %copy-start.2 = (bf16[64,2048]{1,0:T(8,128)(2,1)S(1)}, bf16[64,2048]{1,0:T(8,128)(2,1)}, u32[]{:S(2)}) copy-start(bf16[64,2048]{1,0:T(8,128)(2,1)} %copy-done.1) | copy-start | bytes 786436
  453.7 6.6 slice-start
  457.9 2.8 collective-permute-start.2
  566.7 3.4 copy-start.7
  574.5 6.5 copy-start.8
  574.5 6.6 copy-start.9
  574.5 98.8 %all-to-all-start.5 = ((bf16[16,64,2048]{2,1,0:T(8,128)(2,1)}), bf16[16,64,2048]{2,1,0:T(8,128)(2,1)}, u32[]{:S(2)}, u32[]{:S(2)}) async-start(bf16[16,64,2048]{2,1,0:T(8,128)(2,1)} %bitcast.214), calls=%async_computation.5 | async-start | bytes 8388608 | tf_op jit(solution)/shard_map/all_to_all | solution.py:61
  581.3 103.5 %collective-permute-start.1 = (bf16[64,2048]{1,0:T(8,128)(2,1)}, bf16[64,2048]{1,0:T(8,128)(2,1)}, u32[]{:S(2)}, u32[]{:S(2)}) collective-permute-start(bf16[64,2048]{1,0:T(8,128)(2,1)} %fusion.45), channel_id=1, source_target_pairs={{16,0},{17,1},{18,2},{19,3},{20,4},{21,5},{22,6},{23,7},{24,8},{25... | collective-permute-start | bytes 786440 | tf_op jit(solution)/shard_map/ppermute | solution.py:14
where the time goes:
time: 804 us; the launch traced here: 795 us
  blocking collectives  399 us (50%)
  waiting for transfers between devices  254 us (32%)
  local copies, waits for them, and re-layouts  60.1 us (7%)
  other arithmetic  28.4 us (4%)
  matrix products  26.9 us (3%)
  starting transfers between devices  24.7 us (3%)
    all_to_all x3, blocking collectives, moe_layer(): lax.all_to_all(outgoing, 'expert', split_axis=0, concat_axis=0, tiled=True)  294 us
    all_to_all x3, waiting for transfers between devices, moe_layer(): lax.all_to_all(answered, 'expert', split_axis=0, concat_axis=0, tiled=True)  253 us
    all_gather x1, blocking collectives, local(): lax.all_gather(query_vectors, ('segment', 'expert'), axis=0, tiled=True)  57.1 us
    unnamed x1, blocking collectives  48.3 us
    gather x3, local copies, waits for them, and re-layouts, moe_layer(): returned.reshape(expert_count * capacity, model_width)[target]  24 us
    all_to_all x3, starting transfers between devices, moe_layer(): lax.all_to_all(answered, 'expert', split_axis=0, concat_axis=0, tiled=True)  19.6 us
    scatter x3, local copies, waits for them, and re-layouts, moe_layer(): jnp.zeros((expert_count * capacity, model_width), jnp.bfloat16).at[target]  18.9 us
  transfers between devices with their start and end apart: 6, of which 5 were waited for; matrix products, arithmetic and copies ran while one was open for 4% of the time, Pallas kernels for 0%

commit v1 on v0

--- a/solution.py
+++ b/solution.py
@@ -58,7 +58,15 @@
         gate_up,
         down_proj,
     )
-    returned = lax.all_to_all(answered, "expert", split_axis=0, concat_axis=0, tiled=True)
+    ways, here = (lax.axis_size("expert"), lax.axis_index("expert"))
+    width = answered.shape[0] // ways
+    turned = jnp.roll(answered, -here * width, axis=0)
+    got = [lax.slice_in_dim(turned, 0, width, axis=0)]
+    for far in range(1, ways):
+        sent = lax.slice_in_dim(turned, far * width, (far + 1) * width, axis=0)
+        got.append(lax.ppermute(sent, "expert", [(d, (d + far) % ways) for d in range(ways)]))
+    line = jnp.concatenate(got[::-1], axis=0)
+    returned = jnp.roll(line, (here + 1) * got[0].shape[0], axis=0)
     picked = returned.reshape(expert_count * capacity, model_width)[target].astype(jnp.float32)
     picked = picked.reshape(row_count, top_count, model_width)
     mixture = jnp.sum(picked * gate_weights[:, :, None], axis=1)

time: 804 us -> 892 us (1.11)
  blocking collectives: 399 us -> 116 us
  starting transfers between devices: 24.7 us -> 282 us
  waiting for transfers between devices: 254 us -> 325 us
  local copies, waits for them, and re-layouts: 60.1 us -> 83.3 us
  other arithmetic: 28.4 us -> 47 us
    all_to_all x3 -> x0, blocking collectives: 294 us -> none  [moe_layer(): lax.all_to_all(outgoing, 'expert', split_axis=0, concat_axis=0, tiled=True)]
    ppermute x0 -> x45, starting transfers between devices: none -> 251 us  [moe_layer(): lax.ppermute(sent, 'expert', [(d, (d + far) % ways) for d in range(ways)])]
    ppermute x0 -> x45, waiting for transfers between devices: none -> 59.1 us  [moe_layer(): lax.ppermute(sent, 'expert', [(d, (d + far) % ways) for d in range(ways)])]
    concatenate x0 -> x6, other arithmetic: none -> 13.3 us  [the longest x3 8.6 us: moe_layer(): returned = jnp.roll(line, (here + 1) * got[0].shape[0], axis=0)]
    unnamed x22 -> x103, local copies, waits for them, and re-layouts: 1.53 us -> 14 us
    all_gather x1, blocking collectives: 57.1 us -> 69.3 us  [local(): lax.all_gather(query_vectors, ('segment', 'expert'), axis=0, tiled=True)]
    all_to_all x3, waiting for transfers between devices: 253 us -> 265 us  [moe_layer(): lax.all_to_all(outgoing, 'expert', split_axis=0, concat_axis=0, tiled=True)]
  transfers between devices with their start and end apart: 6 -> 51, of which waited for: 5 -> 21; matrix products, arithmetic and copies ran while one was open for 4% -> 7% of each run, Pallas kernels for 0% -> 0%
where the time goes in v1:
time: 892 us; the launch traced here: 882 us
  waiting for transfers between devices  325 us (36%)
  starting transfers between devices  282 us (32%)
  blocking collectives  116 us (13%)
  local copies, waits for them, and re-layouts  83.3 us (9%)
  other arithmetic  47 us (5%)
  matrix products  26.7 us (3%)
    all_to_all x3, waiting for transfers between devices, moe_layer(): lax.all_to_all(outgoing, 'expert', split_axis=0, concat_axis=0, tiled=True)  265 us
    ppermute x45, starting transfers between devices, moe_layer(): lax.ppermute(sent, 'expert', [(d, (d + far) % ways) for d in range(ways)])  251 us
    all_gather x1, blocking collectives, local(): lax.all_gather(query_vectors, ('segment', 'expert'), axis=0, tiled=True)  69.3 us
    ppermute x45, waiting for transfers between devices, moe_layer(): lax.ppermute(sent, 'expert', [(d, (d + far) % ways) for d in range(ways)])  59.1 us
    unnamed x1, blocking collectives  46.5 us
    all_to_all x3, starting transfers between devices, moe_layer(): lax.all_to_all(outgoing, 'expert', split_axis=0, concat_axis=0, tiled=True)  26.4 us
    gather x3, local copies, waits for them, and re-layouts, moe_layer(): returned.reshape(expert_count * capacity, model_width)[target]  24 us
    scatter x3, local copies, waits for them, and re-layouts, moe_layer(): jnp.zeros((expert_count * capacity, model_width), jnp.bfloat16).at[target]  19.4 us
  transfers between devices with their start and end apart: 51, of which 21 were waited for; matrix products, arithmetic and copies ran while one was open for 7% of the time, Pallas kernels for 0%

profile of v1, /device:TPU:14, one launch (start us, length us, event | category | flops | bytes accessed | tf_op | source)
XLA Modules:
  0.0 882.3 jit_solution(17860870679141251009)
XLA Ops:
  7.1 6.2 scatter_custom_fusion
  13.3 7.3 all-to-all-start
  22.0 3.9 gather_fusion.3
  27.5 87.8 %all-to-all-done = bf16[16,64,2048]{2,1,0:T(8,128)(2,1)} async-done(((bf16[16,64,2048]{2,1,0:T(8,128)(2,1)}), bf16[16,64,2048]{2,1,0:T(8,128)(2,1)}, u32[]{:S(2)}, u32[]{:S(2)}) %all-to-all-start) | async-done | bytes 4194336 | tf_op jit(solution)/shard_map/all_to_all | solution.py:57
  115.3 5.3 fusion.13
  120.6 2.4 convolution_convert_fusion.2
  129.0 2.2 reduce-window.24
  135.5 4.1 collective-permute-start.3
  140.7 3.1 collective-permute-start.5
  147.2 3.8 collective-permute-start.7
  151.0 4.0 collective-permute-start.8
  155.1 5.0 collective-permute-done.4
  160.1 38.7 %collective-permute-start.9 = (bf16[1,64,2048]{2,1,0:T(8,128)(2,1)}, bf16[1,64,2048]{2,1,0:T(8,128)(2,1)S(1)}, u32[]{:S(2)}, u32[]{:S(2)}) collective-permute-start(bf16[1,64,2048]{2,1,0:T(8,128)(2,1)} %get-tuple-element.55), channel_id=1, source_target_pairs={{0,6},{1,7},{2,8},{3,9},{4,10},{5,11},{6,12},{7,13},{8,14},{9,15},... | collective-permute-start | bytes 786440 | tf_op jit(solution)/shard_map/ppermute | solution.py:67
  199.0 7.9 collective-permute-start.12
  207.0 11.2 %collective-permute-start.13 = (bf16[1,64,2048]{2,1,0:T(8,128)(2,1)S(1)}, bf16[1,64,2048]{2,1,0:T(8,128)(2,1)S(1)}, u32[]{:S(2)}, u32[]{:S(2)}) collective-permute-start(bf16[1,64,2048]{2,1,0:T(8,128)(2,1)S(1)} %copy-done.6), channel_id=1, source_target_pairs={{0,2},{1,3},{2,4},{3,5},{4,6},{5,7},{6,8},{7,9},{8,10},{9,11},{10,... | collective-permute-start | bytes 786440 | tf_op jit(solution)/shard_map/ppermute | solution.py:67
  218.2 7.0 collective-permute-start.14
  226.8 3.3 collective-permute-done.12
  230.1 2.7 collective-permute-done.13
  232.8 2.8 collective-permute-done.14
  236.6 2.9 fusion.4
  239.5 8.0 gather_fusion
  247.4 3.4 fusion.8
  257.3 6.6 scatter_custom_fusion.1
  263.9 8.3 all-to-all-start.1
  273.3 2.2 reduce-window.26
  276.0 3.9 gather_fusion.4
  280.1 88.1 %all-to-all-done.1 = bf16[16,64,2048]{2,1,0:T(8,128)(2,1)} async-done(((bf16[16,64,2048]{2,1,0:T(8,128)(2,1)}), bf16[16,64,2048]{2,1,0:T(8,128)(2,1)}, u32[]{:S(2)}, u32[]{:S(2)}) %all-to-all-start.1) | async-done | bytes 4194336 | tf_op jit(solution)/shard_map/all_to_all | solution.py:57
  368.2 5.3 fusion.11
  373.5 2.4 convolution_convert_fusion.1
  382.0 4.2 collective-permute-start.19
  387.2 8.4 collective-permute-done.16
  396.5 2.8 collective-permute-start.22
  400.3 2.3 collective-permute-start.23
  402.7 3.1 collective-permute-start.24
  405.8 6.0 collective-permute-done.20
  411.8 36.6 %collective-permute-start.25 = (bf16[1,64,2048]{2,1,0:T(8,128)(2,1)}, bf16[1,64,2048]{2,1,0:T(8,128)(2,1)S(1)}, u32[]{:S(2)}, u32[]{:S(2)}) collective-permute-start(bf16[1,64,2048]{2,1,0:T(8,128)(2,1)} %get-tuple-element.40), channel_id=1, source_target_pairs={{0,6},{1,7},{2,8},{3,9},{4,10},{5,11},{6,12},{7,13},{8,14},{9,15},... | collective-permute-start | bytes 786440 | tf_op jit(solution)/shard_map/ppermute | solution.py:67
  448.7 19.1 %collective-permute-start.28 = (bf16[1,64,2048]{2,1,0:T(8,128)(2,1)}, bf16[1,64,2048]{2,1,0:T(8,128)(2,1)S(1)}, u32[]{:S(2)}, u32[]{:S(2)}) collective-permute-start(bf16[1,64,2048]{2,1,0:T(8,128)(2,1)} %get-tuple-element.37), channel_id=1, source_target_pairs={{0,3},{1,4},{2,5},{3,6},{4,7},{5,8},{6,9},{7,10},{8,11},{9,12},{10... | collective-permute-start | bytes 786440 | tf_op jit(solution)/shard_map/ppermute | solution.py:67
  467.9 5.6 collective-permute-start.29
  473.5 7.2 collective-permute-start.30
  482.1 4.5 collective-permute-done.29
  486.6 4.2 collective-permute-done.30
  491.9 2.9 fusion.2
  494.7 8.0 gather_fusion.1
  502.8 3.4 fusion.7
  511.8 6.6 scatter_custom_fusion.2
  518.4 10.8 %all-to-all-start.2 = ((bf16[16,64,2048]{2,1,0:T(8,128)(2,1)}), bf16[16,64,2048]{2,1,0:T(8,128)(2,1)}, u32[]{:S(2)}, u32[]{:S(2)}) async-start(bf16[16,64,2048]{2,1,0:T(8,128)(2,1)} %bitcast.215), calls=%async_computation.2 | async-start | bytes 8388608 | tf_op jit(solution)/shard_map/all_to_all | solution.py:57
  532.3 3.9 gather_fusion.5
  536.4 89.0 %all-to-all-done.2 = bf16[16,64,2048]{2,1,0:T(8,128)(2,1)} async-done(((bf16[16,64,2048]{2,1,0:T(8,128)(2,1)}), bf16[16,64,2048]{2,1,0:T(8,128)(2,1)}, u32[]{:S(2)}, u32[]{:S(2)}) %all-to-all-start.2) | async-done | bytes 4194336 | tf_op jit(solution)/shard_map/all_to_all | solution.py:57
  625.3 5.3 fusion.9
  630.7 2.4 convolution_convert_fusion
  638.7 4.3 collective-permute-start.36
  643.1 9.8 %collective-permute-done.33 = bf16[1,64,2048]{2,1,0:T(8,128)(2,1)} collective-permute-done((bf16[1,64,2048]{2,1,0:T(8,128)(2,1)}, bf16[1,64,2048]{2,1,0:T(8,128)(2,1)}, u32[]{:S(2)}, u32[]{:S(2)}) %collective-permute-start.33) | collective-permute-done | bytes 262176 | tf_op jit(solution)/shard_map/ppermute | solution.py:67
  655.1 6.8 collective-permute-start.39
  661.9 17.0 %collective-permute-start.40 = (bf16[1,64,2048]{2,1,0:T(8,128)(2,1)}, bf16[1,64,2048]{2,1,0:T(8,128)(2,1)S(1)}, u32[]{:S(2)}, u32[]{:S(2)}) collective-permute-start(bf16[1,64,2048]{2,1,0:T(8,128)(2,1)} %get-tuple-element.27), channel_id=1, source_target_pairs={{0,8},{1,9},{2,10},{3,11},{4,12},{5,13},{6,14},{7,15},{8,0},{9,1},... | collective-permute-start | bytes 786440 | tf_op jit(solution)/shard_map/ppermute | solution.py:67
  679.1 18.2 %collective-permute-start.42 = (bf16[1,64,2048]{2,1,0:T(8,128)(2,1)}, bf16[1,64,2048]{2,1,0:T(8,128)(2,1)S(1)}, u32[]{:S(2)}, u32[]{:S(2)}) collective-permute-start(bf16[1,64,2048]{2,1,0:T(8,128)(2,1)} %get-tuple-element.25), channel_id=1, source_target_pairs={{0,6},{1,7},{2,8},{3,9},{4,10},{5,11},{6,12},{7,13},{8,14},{9,15},... | collective-permute-start | bytes 786440 | tf_op jit(solution)/shard_map/ppermute | solution.py:67
  697.3 19.7 %collective-permute-start.43 = (bf16[1,64,2048]{2,1,0:T(8,128)(2,1)}, bf16[1,64,2048]{2,1,0:T(8,128)(2,1)S(1)}, u32[]{:S(2)}, u32[]{:S(2)}) collective-permute-start(bf16[1,64,2048]{2,1,0:T(8,128)(2,1)} %get-tuple-element.24), channel_id=1, source_target_pairs={{0,5},{1,6},{2,7},{3,8},{4,9},{5,10},{6,11},{7,12},{8,13},{9,14},{... | collective-permute-start | bytes 786440 | tf_op jit(solution)/shard_map/ppermute | solution.py:67
  717.2 17.5 %collective-permute-start.46 = (bf16[1,64,2048]{2,1,0:T(8,128)(2,1)S(1)}, bf16[1,64,2048]{2,1,0:T(8,128)(2,1)S(1)}, u32[]{:S(2)}, u32[]{:S(2)}) collective-permute-start(bf16[1,64,2048]{2,1,0:T(8,128)(2,1)S(1)} %copy-done.9), channel_id=1, source_target_pairs={{0,2},{1,3},{2,4},{3,5},{4,6},{5,7},{6,8},{7,9},{8,10},{9,11},{10,... | collective-permute-start | bytes 786440 | tf_op jit(solution)/shard_map/ppermute | solution.py:67
  737.3 5.6 collective-permute-done.46
  743.0 3.3 collective-permute-done.47
  747.2 2.9 fusion
  750.1 8.0 gather_fusion.2
  758.1 3.4 fusion.6
  763.6 69.3 %all-gather = bf16[32,2,2048]{2,1,0:T(2,128)(2,1)S(1)} all-gather(bf16[1,2,2048]{2,1,0:T(2,128)(2,1)S(1)} %slice_bitcast_fusion), channel_id=1, replica_groups=mesh['segment'=2,'expert'=16] {'segment','expert'}, dimensions={0}, use_global_device_ids=true | all-gather | bytes 270336 | tf_op jit(solution)/shard_map/all_gather | solution.py:120
  834.8 46.5 %all-reduce.2 = (f32[64]{0:T(128)S(1)}, f32[64]{0:T(128)S(1)}) all-reduce(f32[64]{0:T(128)S(1)} %get-tuple-element.5, f32[64]{0:T(128)S(1)} %get-tuple-element.4), channel_id=3, replica_groups=mesh['segment'=2,'expert'=16] {'segment','expert'}, use_global_device_ids=true, to_apply=%region_27.30.clone | all-reduce | flops 128 | bytes 1024
  (262 shorter events, 71.5 us)
Async XLA Ops:
  0.6 114.6 %copy-start = (bf16[1,1,2048,768]{3,2,1,0:T(8,128)(2,1)S(1)}, bf16[1,1,2048,768]{3,2,1,0:T(8,128)(2,1)}, u32[]{:S(2)}) copy-start(bf16[1,1,2048,768]{3,2,1,0:T(8,128)(2,1)} %param.16) | copy-start | bytes 9437188
  2.1 24.1 %copy-start.12 = (s32[1,1,64,8]{2,3,1,0:T(8,128)}, s32[1,1,64,8]{2,3,1,0:T(8,128)S(1)}, u32[]{:S(2)}) copy-start(s32[1,1,64,8]{2,3,1,0:T(8,128)S(1)} %get-tuple-element.68) | copy-start | bytes 6148
  13.3 101.9 %all-to-all-start = ((bf16[16,64,2048]{2,1,0:T(8,128)(2,1)}), bf16[16,64,2048]{2,1,0:T(8,128)(2,1)}, u32[]{:S(2)}, u32[]{:S(2)}) async-start(bf16[16,64,2048]{2,1,0:T(8,128)(2,1)} %bitcast.214), calls=%async_computation | async-start | bytes 8388608 | tf_op jit(solution)/shard_map/all_to_all | solution.py:57
  128.3 12.4 %collective-permute-start = (bf16[1,64,2048]{2,1,0:T(8,128)(2,1)}, bf16[1,64,2048]{2,1,0:T(8,128)(2,1)}, u32[]{:S(2)}, u32[]{:S(2)}) collective-permute-start(bf16[1,64,2048]{2,1,0:T(8,128)(2,1)} %get-tuple-element.64), channel_id=1, source_target_pairs={{0,15},{1,0},{2,1},{3,2},{4,3},{5,4},{6,5},{7,6},{8,7},{9,8},{10,9... | collective-permute-start | bytes 786440 | tf_op jit(solution)/shard_map/ppermute | solution.py:67
  132.0 12.8 %collective-permute-start.1 = (bf16[1,64,2048]{2,1,0:T(8,128)(2,1)}, bf16[1,64,2048]{2,1,0:T(8,128)(2,1)}, u32[]{:S(2)}, u32[]{:S(2)}) collective-permute-start(bf16[1,64,2048]{2,1,0:T(8,128)(2,1)} %get-tuple-element.63), channel_id=1, source_target_pairs={{0,14},{1,15},{2,0},{3,1},{4,2},{5,3},{6,4},{7,5},{8,6},{9,7},{10,... | collective-permute-start | bytes 786440 | tf_op jit(solution)/shard_map/ppermute | solution.py:67
  135.4 101.1 %copy-start.19 = (s32[16,5]{0,1:T(8,128)}, s32[16,5]{0,1:T(8,128)S(1)}, u32[]{:S(2)}) copy-start(s32[16,5]{0,1:T(8,128)S(1)} %reduce-window.25) | copy-start | bytes 964
  135.4 71.5 %copy-start.6 = (bf16[1,64,2048]{2,1,0:T(8,128)(2,1)S(1)}, bf16[1,64,2048]{2,1,0:T(8,128)(2,1)}, u32[]{:S(2)}) copy-start(bf16[1,64,2048]{2,1,0:T(8,128)(2,1)} %get-tuple-element.51) | copy-start | bytes 786436
  135.4 11.8 %collective-permute-start.2 = (bf16[1,64,2048]{2,1,0:T(8,128)(2,1)}, bf16[1,64,2048]{2,1,0:T(8,128)(2,1)S(1)}, u32[]{:S(2)}, u32[]{:S(2)}) collective-permute-start(bf16[1,64,2048]{2,1,0:T(8,128)(2,1)} %get-tuple-element.62), channel_id=1, source_target_pairs={{0,13},{1,14},{2,15},{3,0},{4,1},{5,2},{6,3},{7,4},{8,5},{9,6},{10... | collective-permute-start | bytes 786440 | tf_op jit(solution)/shard_map/ppermute | solution.py:67
  135.5 15.5 %collective-permute-start.3 = (bf16[1,64,2048]{2,1,0:T(8,128)(2,1)}, bf16[1,64,2048]{2,1,0:T(8,128)(2,1)S(1)}, u32[]{:S(2)}, u32[]{:S(2)}) collective-permute-start(bf16[1,64,2048]{2,1,0:T(8,128)(2,1)} %get-tuple-element.61), channel_id=1, source_target_pairs={{0,12},{1,13},{2,14},{3,15},{4,0},{5,1},{6,2},{7,3},{8,4},{9,5},{1... | collective-permute-start | bytes 786440 | tf_op jit(solution)/shard_map/ppermute | solution.py:67
  139.6 20.5 %collective-permute-start.4 = (bf16[1,64,2048]{2,1,0:T(8,128)(2,1)}, bf16[1,64,2048]{2,1,0:T(8,128)(2,1)S(1)}, u32[]{:S(2)}, u32[]{:S(2)}) collective-permute-start(bf16[1,64,2048]{2,1,0:T(8,128)(2,1)} %get-tuple-element.60), channel_id=1, source_target_pairs={{0,11},{1,12},{2,13},{3,14},{4,15},{5,0},{6,1},{7,2},{8,3},{9,4},{... | collective-permute-start | bytes 786440 | tf_op jit(solution)/shard_map/ppermute | solution.py:67
  140.7 58.1 %collective-permute-start.5 = (bf16[1,64,2048]{2,1,0:T(8,128)(2,1)}, bf16[1,64,2048]{2,1,0:T(8,128)(2,1)S(1)}, u32[]{:S(2)}, u32[]{:S(2)}) collective-permute-start(bf16[1,64,2048]{2,1,0:T(8,128)(2,1)} %get-tuple-element.59), channel_id=1, source_target_pairs={{0,10},{1,11},{2,12},{3,13},{4,14},{5,15},{6,0},{7,1},{8,2},{9,3},... | collective-permute-start | bytes 786440 | tf_op jit(solution)/shard_map/ppermute | solution.py:67
  144.8 54.1 %collective-permute-start.6 = (bf16[1,64,2048]{2,1,0:T(8,128)(2,1)}, bf16[1,64,2048]{2,1,0:T(8,128)(2,1)S(1)}, u32[]{:S(2)}, u32[]{:S(2)}) collective-permute-start(bf16[1,64,2048]{2,1,0:T(8,128)(2,1)} %get-tuple-element.58), channel_id=1, source_target_pairs={{0,9},{1,10},{2,11},{3,12},{4,13},{5,14},{6,15},{7,0},{8,1},{9,2},... | collective-permute-start | bytes 786440 | tf_op jit(solution)/shard_map/ppermute | solution.py:67
  147.2 51.8 %collective-permute-start.7 = (bf16[1,64,2048]{2,1,0:T(8,128)(2,1)}, bf16[1,64,2048]{2,1,0:T(8,128)(2,1)S(1)}, u32[]{:S(2)}, u32[]{:S(2)}) collective-permute-start(bf16[1,64,2048]{2,1,0:T(8,128)(2,1)} %get-tuple-element.57), channel_id=1, source_target_pairs={{0,8},{1,9},{2,10},{3,11},{4,12},{5,13},{6,14},{7,15},{8,0},{9,1},... | collective-permute-start | bytes 786440 | tf_op jit(solution)/shard_map/ppermute | solution.py:67
  151.0 55.9 %collective-permute-start.8 = (bf16[1,64,2048]{2,1,0:T(8,128)(2,1)}, bf16[1,64,2048]{2,1,0:T(8,128)(2,1)S(1)}, u32[]{:S(2)}, u32[]{:S(2)}) collective-permute-start(bf16[1,64,2048]{2,1,0:T(8,128)(2,1)} %get-tuple-element.56), channel_id=1, source_target_pairs={{0,7},{1,8},{2,9},{3,10},{4,11},{5,12},{6,13},{7,14},{8,15},{9,0},... | collective-permute-start | bytes 786440 | tf_op jit(solution)/shard_map/ppermute | solution.py:67
  160.1 58.1 %collective-permute-start.9 = (bf16[1,64,2048]{2,1,0:T(8,128)(2,1)}, bf16[1,64,2048]{2,1,0:T(8,128)(2,1)S(1)}, u32[]{:S(2)}, u32[]{:S(2)}) collective-permute-start(bf16[1,64,2048]{2,1,0:T(8,128)(2,1)} %get-tuple-element.55), channel_id=1, source_target_pairs={{0,6},{1,7},{2,8},{3,9},{4,10},{5,11},{6,12},{7,13},{8,14},{9,15},... | collective-permute-start | bytes 786440 | tf_op jit(solution)/shard_map/ppermute | solution.py:67
  198.8 26.5 %collective-permute-start.10 = (bf16[1,64,2048]{2,1,0:T(8,128)(2,1)}, bf16[1,64,2048]{2,1,0:T(8,128)(2,1)S(1)}, u32[]{:S(2)}, u32[]{:S(2)}) collective-permute-start(bf16[1,64,2048]{2,1,0:T(8,128)(2,1)} %get-tuple-element.54), channel_id=1, source_target_pairs={{0,5},{1,6},{2,7},{3,8},{4,9},{5,10},{6,11},{7,12},{8,13},{9,14},{... | collective-permute-start | bytes 786440 | tf_op jit(solution)/shard_map/ppermute | solution.py:67
  198.9 27.9 %collective-permute-start.11 = (bf16[1,64,2048]{2,1,0:T(8,128)(2,1)}, bf16[1,64,2048]{2,1,0:T(8,128)(2,1)S(1)}, u32[]{:S(2)}, u32[]{:S(2)}) collective-permute-start(bf16[1,64,2048]{2,1,0:T(8,128)(2,1)} %get-tuple-element.53), channel_id=1, source_target_pairs={{0,4},{1,5},{2,6},{3,7},{4,8},{5,9},{6,10},{7,11},{8,12},{9,13},{1... | collective-permute-start | bytes 786440 | tf_op jit(solution)/shard_map/ppermute | solution.py:67
  199.0 31.1 %collective-permute-start.12 = (bf16[1,64,2048]{2,1,0:T(8,128)(2,1)}, bf16[1,64,2048]{2,1,0:T(8,128)(2,1)S(1)}, u32[]{:S(2)}, u32[]{:S(2)}) collective-permute-start(bf16[1,64,2048]{2,1,0:T(8,128)(2,1)} %get-tuple-element.52), channel_id=1, source_target_pairs={{0,3},{1,4},{2,5},{3,6},{4,7},{5,8},{6,9},{7,10},{8,11},{9,12},{10... | collective-permute-start | bytes 786440 | tf_op jit(solution)/shard_map/ppermute | solution.py:67
  207.0 25.8 %collective-permute-start.13 = (bf16[1,64,2048]{2,1,0:T(8,128)(2,1)S(1)}, bf16[1,64,2048]{2,1,0:T(8,128)(2,1)S(1)}, u32[]{:S(2)}, u32[]{:S(2)}) collective-permute-start(bf16[1,64,2048]{2,1,0:T(8,128)(2,1)S(1)} %copy-done.6), channel_id=1, source_target_pairs={{0,2},{1,3},{2,4},{3,5},{4,6},{5,7},{6,8},{7,9},{8,10},{9,11},{10,... | collective-permute-start | bytes 786440 | tf_op jit(solution)/shard_map/ppermute | solution.py:67
  218.2 17.4 %collective-permute-start.14 = (bf16[1,64,2048]{2,1,0:T(8,128)(2,1)S(1)}, bf16[1,64,2048]{2,1,0:T(8,128)(2,1)S(1)}, u32[]{:S(2)}, u32[]{:S(2)}) collective-permute-start(bf16[1,64,2048]{2,1,0:T(8,128)(2,1)S(1)} %get-tuple-element.50), channel_id=1, source_target_pairs={{0,1},{1,2},{2,3},{3,4},{4,5},{5,6},{6,7},{7,8},{8,9},{9,10},{10,1... | collective-permute-start | bytes 786440 | tf_op jit(solution)/shard_map/ppermute | solution.py:67
  239.4 14.5 %slice-start = ((s32[16,5]{0,1:T(8,128)}), s32[16,4]{0,1:T(4,128)S(1)}, s32[]{:S(2)}) async-start(s32[16,5]{0,1:T(8,128)} %copy-done.19), calls=%async_computation.3 | async-start | bytes 4096 | tf_op jit(solution)/shard_map/slice.3
  239.4 14.5 %copy-start.21 = (s32[512]{0:T(512)S(1)}, s32[512]{0:T(512)}, u32[]{:S(2)}) copy-start(s32[512]{0:T(512)} %eq.118) | copy-start | bytes 6148
  239.5 14.6 %copy-start.17 = (s32[1,1,64,8]{2,3,1,0:T(8,128)S(1)}, s32[1,1,64,8]{2,3,1,0:T(8,128)}, u32[]{:S(2)}) copy-start(s32[1,1,64,8]{2,3,1,0:T(8,128)} %get-tuple-element.70) | copy-start | bytes 6148
  252.6 2.6 collective-permute-start.15
  263.9 104.3 %all-to-all-start.1 = ((bf16[16,64,2048]{2,1,0:T(8,128)(2,1)}), bf16[16,64,2048]{2,1,0:T(8,128)(2,1)}, u32[]{:S(2)}, u32[]{:S(2)}) async-start(bf16[16,64,2048]{2,1,0:T(8,128)(2,1)} %bitcast.216), calls=%async_computation.1 | async-start | bytes 8388608 | tf_op jit(solution)/shard_map/all_to_all | solution.py:57
  381.2 14.3 %collective-permute-start.16 = (bf16[1,64,2048]{2,1,0:T(8,128)(2,1)}, bf16[1,64,2048]{2,1,0:T(8,128)(2,1)}, u32[]{:S(2)}, u32[]{:S(2)}) collective-permute-start(bf16[1,64,2048]{2,1,0:T(8,128)(2,1)} %get-tuple-element.49), channel_id=1, source_target_pairs={{0,15},{1,0},{2,1},{3,2},{4,3},{5,4},{6,5},{7,6},{8,7},{9,8},{10,9... | collective-permute-start | bytes 786440 | tf_op jit(solution)/shard_map/ppermute | solution.py:67
  381.2 15.3 %collective-permute-start.17 = (bf16[1,64,2048]{2,1,0:T(8,128)(2,1)}, bf16[1,64,2048]{2,1,0:T(8,128)(2,1)}, u32[]{:S(2)}, u32[]{:S(2)}) collective-permute-start(bf16[1,64,2048]{2,1,0:T(8,128)(2,1)} %get-tuple-element.48), channel_id=1, source_target_pairs={{0,14},{1,15},{2,0},{3,1},{4,2},{5,3},{6,4},{7,5},{8,6},{9,7},{10,... | collective-permute-start | bytes 786440 | tf_op jit(solution)/shard_map/ppermute | solution.py:67
  382.0 85.8 %copy-start.8 = (bf16[1,64,2048]{2,1,0:T(8,128)(2,1)S(1)}, bf16[1,64,2048]{2,1,0:T(8,128)(2,1)}, u32[]{:S(2)}) copy-start(bf16[1,64,2048]{2,1,0:T(8,128)(2,1)} %get-tuple-element.36) | copy-start | bytes 786436
  382.0 18.3 %collective-permute-start.18 = (bf16[1,64,2048]{2,1,0:T(8,128)(2,1)}, bf16[1,64,2048]{2,1,0:T(8,128)(2,1)S(1)}, u32[]{:S(2)}, u32[]{:S(2)}) collective-permute-start(bf16[1,64,2048]{2,1,0:T(8,128)(2,1)} %get-tuple-element.47), channel_id=1, source_target_pairs={{0,13},{1,14},{2,15},{3,0},{4,1},{5,2},{6,3},{7,4},{8,5},{9,6},{10... | collective-permute-start | bytes 786440 | tf_op jit(solution)/shard_map/ppermute | solution.py:67
  382.0 20.6 %collective-permute-start.19 = (bf16[1,64,2048]{2,1,0:T(8,128)(2,1)}, bf16[1,64,2048]{2,1,0:T(8,128)(2,1)S(1)}, u32[]{:S(2)}, u32[]{:S(2)}) collective-permute-start(bf16[1,64,2048]{2,1,0:T(8,128)(2,1)} %get-tuple-element.46), channel_id=1, source_target_pairs={{0,12},{1,13},{2,14},{3,15},{4,0},{5,1},{6,2},{7,3},{8,4},{9,5},{1... | collective-permute-start | bytes 786440 | tf_op jit(solution)/shard_map/ppermute | solution.py:67
  386.3 25.6 %collective-permute-start.20 = (bf16[1,64,2048]{2,1,0:T(8,128)(2,1)}, bf16[1,64,2048]{2,1,0:T(8,128)(2,1)S(1)}, u32[]{:S(2)}, u32[]{:S(2)}) collective-permute-start(bf16[1,64,2048]{2,1,0:T(8,128)(2,1)} %get-tuple-element.45), channel_id=1, source_target_pairs={{0,11},{1,12},{2,13},{3,14},{4,15},{5,0},{6,1},{7,2},{8,3},{9,4},{... | collective-permute-start | bytes 786440 | tf_op jit(solution)/shard_map/ppermute | solution.py:67
  395.6 52.9 %collective-permute-start.21 = (bf16[1,64,2048]{2,1,0:T(8,128)(2,1)}, bf16[1,64,2048]{2,1,0:T(8,128)(2,1)S(1)}, u32[]{:S(2)}, u32[]{:S(2)}) collective-permute-start(bf16[1,64,2048]{2,1,0:T(8,128)(2,1)} %get-tuple-element.44), channel_id=1, source_target_pairs={{0,10},{1,11},{2,12},{3,13},{4,14},{5,15},{6,0},{7,1},{8,2},{9,3},... | collective-permute-start | bytes 786440 | tf_op jit(solution)/shard_map/ppermute | solution.py:67
  396.5 52.0 %collective-permute-start.22 = (bf16[1,64,2048]{2,1,0:T(8,128)(2,1)}, bf16[1,64,2048]{2,1,0:T(8,128)(2,1)S(1)}, u32[]{:S(2)}, u32[]{:S(2)}) collective-permute-start(bf16[1,64,2048]{2,1,0:T(8,128)(2,1)} %get-tuple-element.43), channel_id=1, source_target_pairs={{0,9},{1,10},{2,11},{3,12},{4,13},{5,14},{6,15},{7,0},{8,1},{9,2},... | collective-permute-start | bytes 786440 | tf_op jit(solution)/shard_map/ppermute | solution.py:67
  400.3 48.4 %collective-permute-start.23 = (bf16[1,64,2048]{2,1,0:T(8,128)(2,1)}, bf16[1,64,2048]{2,1,0:T(8,128)(2,1)S(1)}, u32[]{:S(2)}, u32[]{:S(2)}) collective-permute-start(bf16[1,64,2048]{2,1,0:T(8,128)(2,1)} %get-tuple-element.42), channel_id=1, source_target_pairs={{0,8},{1,9},{2,10},{3,11},{4,12},{5,13},{6,14},{7,15},{8,0},{9,1},... | collective-permute-start | bytes 786440 | tf_op jit(solution)/shard_map/ppermute | solution.py:67
  402.7 65.2 %collective-permute-start.24 = (bf16[1,64,2048]{2,1,0:T(8,128)(2,1)}, bf16[1,64,2048]{2,1,0:T(8,128)(2,1)S(1)}, u32[]{:S(2)}, u32[]{:S(2)}) collective-permute-start(bf16[1,64,2048]{2,1,0:T(8,128)(2,1)} %get-tuple-element.41), channel_id=1, source_target_pairs={{0,7},{1,8},{2,9},{3,10},{4,11},{5,12},{6,13},{7,14},{8,15},{9,0},... | collective-permute-start | bytes 786440 | tf_op jit(solution)/shard_map/ppermute | solution.py:67
  411.8 61.7 %collective-permute-start.25 = (bf16[1,64,2048]{2,1,0:T(8,128)(2,1)}, bf16[1,64,2048]{2,1,0:T(8,128)(2,1)S(1)}, u32[]{:S(2)}, u32[]{:S(2)}) collective-permute-start(bf16[1,64,2048]{2,1,0:T(8,128)(2,1)} %get-tuple-element.40), channel_id=1, source_target_pairs={{0,6},{1,7},{2,8},{3,9},{4,10},{5,11},{6,12},{7,13},{8,14},{9,15},... | collective-permute-start | bytes 786440 | tf_op jit(solution)/shard_map/ppermute | solution.py:67
  448.5 32.3 %collective-permute-start.26 = (bf16[1,64,2048]{2,1,0:T(8,128)(2,1)}, bf16[1,64,2048]{2,1,0:T(8,128)(2,1)S(1)}, u32[]{:S(2)}, u32[]{:S(2)}) collective-permute-start(bf16[1,64,2048]{2,1,0:T(8,128)(2,1)} %get-tuple-element.39), channel_id=1, source_target_pairs={{0,5},{1,6},{2,7},{3,8},{4,9},{5,10},{6,11},{7,12},{8,13},{9,14},{... | collective-permute-start | bytes 786440 | tf_op jit(solution)/shard_map/ppermute | solution.py:67
  448.6 33.5 %collective-permute-start.27 = (bf16[1,64,2048]{2,1,0:T(8,128)(2,1)}, bf16[1,64,2048]{2,1,0:T(8,128)(2,1)S(1)}, u32[]{:S(2)}, u32[]{:S(2)}) collective-permute-start(bf16[1,64,2048]{2,1,0:T(8,128)(2,1)} %get-tuple-element.38), channel_id=1, source_target_pairs={{0,4},{1,5},{2,6},{3,7},{4,8},{5,9},{6,10},{7,11},{8,12},{9,13},{1... | collective-permute-start | bytes 786440 | tf_op jit(solution)/shard_map/ppermute | solution.py:67
  448.7 33.4 %collective-permute-start.28 = (bf16[1,64,2048]{2,1,0:T(8,128)(2,1)}, bf16[1,64,2048]{2,1,0:T(8,128)(2,1)S(1)}, u32[]{:S(2)}, u32[]{:S(2)}) collective-permute-start(bf16[1,64,2048]{2,1,0:T(8,128)(2,1)} %get-tuple-element.37), channel_id=1, source_target_pairs={{0,3},{1,4},{2,5},{3,6},{4,7},{5,8},{6,9},{7,10},{8,11},{9,12},{10... | collective-permute-start | bytes 786440 | tf_op jit(solution)/shard_map/ppermute | solution.py:67
  467.9 18.7 %collective-permute-start.29 = (bf16[1,64,2048]{2,1,0:T(8,128)(2,1)S(1)}, bf16[1,64,2048]{2,1,0:T(8,128)(2,1)S(1)}, u32[]{:S(2)}, u32[]{:S(2)}) collective-permute-start(bf16[1,64,2048]{2,1,0:T(8,128)(2,1)S(1)} %copy-done.8), channel_id=1, source_target_pairs={{0,2},{1,3},{2,4},{3,5},{4,6},{5,7},{6,8},{7,9},{8,10},{9,11},{10,... | collective-permute-start | bytes 786440 | tf_op jit(solution)/shard_map/ppermute | solution.py:67
  473.5 17.4 %collective-permute-start.30 = (bf16[1,64,2048]{2,1,0:T(8,128)(2,1)S(1)}, bf16[1,64,2048]{2,1,0:T(8,128)(2,1)S(1)}, u32[]{:S(2)}, u32[]{:S(2)}) collective-permute-start(bf16[1,64,2048]{2,1,0:T(8,128)(2,1)S(1)} %get-tuple-element.35), channel_id=1, source_target_pairs={{0,1},{1,2},{2,3},{3,4},{4,5},{5,6},{6,7},{7,8},{8,9},{9,10},{10,1... | collective-permute-start | bytes 786440 | tf_op jit(solution)/shard_map/ppermute | solution.py:67
  494.7 14.2 %slice-start.1 = ((s32[16,5]{0,1:T(8,128)}), s32[16,4]{0,1:T(4,128)S(1)}, s32[]{:S(2)}) async-start(s32[16,5]{0,1:T(8,128)} %copy-done.20), calls=%async_computation.4 | async-start | bytes 4096 | tf_op jit(solution)/shard_map/slice.5
  494.7 14.3 %copy-start.16 = (s32[1,1,64,8]{2,3,1,0:T(8,128)S(1)}, s32[1,1,64,8]{2,3,1,0:T(8,128)}, u32[]{:S(2)}) copy-start(s32[1,1,64,8]{2,3,1,0:T(8,128)} %get-tuple-element.69) | copy-start | bytes 6148
  507.0 2.8 collective-permute-start.32
  518.4 106.9 %all-to-all-start.2 = ((bf16[16,64,2048]{2,1,0:T(8,128)(2,1)}), bf16[16,64,2048]{2,1,0:T(8,128)(2,1)}, u32[]{:S(2)}, u32[]{:S(2)}) async-start(bf16[16,64,2048]{2,1,0:T(8,128)(2,1)} %bitcast.215), calls=%async_computation.2 | async-start | bytes 8388608 | tf_op jit(solution)/shard_map/all_to_all | solution.py:57
  529.7 231.8 %collective-permute-start.31 = (bf16[64,2048]{1,0:T(8,128)(2,1)}, bf16[64,2048]{1,0:T(8,128)(2,1)}, u32[]{:S(2)}, u32[]{:S(2)}) collective-permute-start(bf16[64,2048]{1,0:T(8,128)(2,1)} %fusion.51), channel_id=1, source_target_pairs={{16,0},{17,1},{18,2},{19,3},{20,4},{21,5},{22,6},{23,7},{24,8},{25... | collective-permute-start | bytes 786440 | tf_op jit(solution)/shard_map/ppermute | solution.py:14
  638.5 14.4 %collective-permute-start.33 = (bf16[1,64,2048]{2,1,0:T(8,128)(2,1)}, bf16[1,64,2048]{2,1,0:T(8,128)(2,1)}, u32[]{:S(2)}, u32[]{:S(2)}) collective-permute-start(bf16[1,64,2048]{2,1,0:T(8,128)(2,1)} %get-tuple-element.34), channel_id=1, source_target_pairs={{0,15},{1,0},{2,1},{3,2},{4,3},{5,4},{6,5},{7,6},{8,7},{9,8},{10,9... | collective-permute-start | bytes 786440 | tf_op jit(solution)/shard_map/ppermute | solution.py:67
  638.5 15.4 %collective-permute-start.34 = (bf16[1,64,2048]{2,1,0:T(8,128)(2,1)}, bf16[1,64,2048]{2,1,0:T(8,128)(2,1)}, u32[]{:S(2)}, u32[]{:S(2)}) collective-permute-start(bf16[1,64,2048]{2,1,0:T(8,128)(2,1)} %get-tuple-element.33), channel_id=1, source_target_pairs={{0,14},{1,15},{2,0},{3,1},{4,2},{5,3},{6,4},{7,5},{8,6},{9,7},{10,... | collective-permute-start | bytes 786440 | tf_op jit(solution)/shard_map/ppermute | solution.py:67
  638.6 78.4 %copy-start.10 = (bf16[1,64,2048]{2,1,0:T(8,128)(2,1)S(1)}, bf16[1,64,2048]{2,1,0:T(8,128)(2,1)}, u32[]{:S(2)}) copy-start(bf16[1,64,2048]{2,1,0:T(8,128)(2,1)} %get-tuple-element.22) | copy-start | bytes 786436
  638.7 78.5 %copy-start.9 = (bf16[1,64,2048]{2,1,0:T(8,128)(2,1)S(1)}, bf16[1,64,2048]{2,1,0:T(8,128)(2,1)}, u32[]{:S(2)}) copy-start(bf16[1,64,2048]{2,1,0:T(8,128)(2,1)} %get-tuple-element.21) | copy-start | bytes 786436
  638.7 96.1 %copy-start.7 = (bf16[1,64,2048]{2,1,0:T(8,128)(2,1)S(1)}, bf16[1,64,2048]{2,1,0:T(8,128)(2,1)}, u32[]{:S(2)}) copy-start(bf16[1,64,2048]{2,1,0:T(8,128)(2,1)} %get-tuple-element.20) | copy-start | bytes 786436
  638.7 16.4 %collective-permute-start.35 = (bf16[1,64,2048]{2,1,0:T(8,128)(2,1)}, bf16[1,64,2048]{2,1,0:T(8,128)(2,1)S(1)}, u32[]{:S(2)}, u32[]{:S(2)}) collective-permute-start(bf16[1,64,2048]{2,1,0:T(8,128)(2,1)} %get-tuple-element.32), channel_id=1, source_target_pairs={{0,13},{1,14},{2,15},{3,0},{4,1},{5,2},{6,3},{7,4},{8,5},{9,6},{10... | collective-permute-start | bytes 786440 | tf_op jit(solution)/shard_map/ppermute | solution.py:67
  638.7 23.2 %collective-permute-start.36 = (bf16[1,64,2048]{2,1,0:T(8,128)(2,1)}, bf16[1,64,2048]{2,1,0:T(8,128)(2,1)S(1)}, u32[]{:S(2)}, u32[]{:S(2)}) collective-permute-start(bf16[1,64,2048]{2,1,0:T(8,128)(2,1)} %get-tuple-element.31), channel_id=1, source_target_pairs={{0,12},{1,13},{2,14},{3,15},{4,0},{5,1},{6,2},{7,3},{8,4},{9,5},{1... | collective-permute-start | bytes 786440 | tf_op jit(solution)/shard_map/ppermute | solution.py:67
  652.9 26.1 %collective-permute-start.37 = (bf16[1,64,2048]{2,1,0:T(8,128)(2,1)}, bf16[1,64,2048]{2,1,0:T(8,128)(2,1)S(1)}, u32[]{:S(2)}, u32[]{:S(2)}) collective-permute-start(bf16[1,64,2048]{2,1,0:T(8,128)(2,1)} %get-tuple-element.30), channel_id=1, source_target_pairs={{0,11},{1,12},{2,13},{3,14},{4,15},{5,0},{6,1},{7,2},{8,3},{9,4},{... | collective-permute-start | bytes 786440 | tf_op jit(solution)/shard_map/ppermute | solution.py:67
  653.9 25.2 %collective-permute-start.38 = (bf16[1,64,2048]{2,1,0:T(8,128)(2,1)}, bf16[1,64,2048]{2,1,0:T(8,128)(2,1)S(1)}, u32[]{:S(2)}, u32[]{:S(2)}) collective-permute-start(bf16[1,64,2048]{2,1,0:T(8,128)(2,1)} %get-tuple-element.29), channel_id=1, source_target_pairs={{0,10},{1,11},{2,12},{3,13},{4,14},{5,15},{6,0},{7,1},{8,2},{9,3},... | collective-permute-start | bytes 786440 | tf_op jit(solution)/shard_map/ppermute | solution.py:67
  655.1 42.2 %collective-permute-start.39 = (bf16[1,64,2048]{2,1,0:T(8,128)(2,1)}, bf16[1,64,2048]{2,1,0:T(8,128)(2,1)S(1)}, u32[]{:S(2)}, u32[]{:S(2)}) collective-permute-start(bf16[1,64,2048]{2,1,0:T(8,128)(2,1)} %get-tuple-element.28), channel_id=1, source_target_pairs={{0,9},{1,10},{2,11},{3,12},{4,13},{5,14},{6,15},{7,0},{8,1},{9,2},... | collective-permute-start | bytes 786440 | tf_op jit(solution)/shard_map/ppermute | solution.py:67
  661.9 55.1 %collective-permute-start.40 = (bf16[1,64,2048]{2,1,0:T(8,128)(2,1)}, bf16[1,64,2048]{2,1,0:T(8,128)(2,1)S(1)}, u32[]{:S(2)}, u32[]{:S(2)}) collective-permute-start(bf16[1,64,2048]{2,1,0:T(8,128)(2,1)} %get-tuple-element.27), channel_id=1, source_target_pairs={{0,8},{1,9},{2,10},{3,11},{4,12},{5,13},{6,14},{7,15},{8,0},{9,1},... | collective-permute-start | bytes 786440 | tf_op jit(solution)/shard_map/ppermute | solution.py:67
  679.0 38.1 %collective-permute-start.41 = (bf16[1,64,2048]{2,1,0:T(8,128)(2,1)}, bf16[1,64,2048]{2,1,0:T(8,128)(2,1)S(1)}, u32[]{:S(2)}, u32[]{:S(2)}) collective-permute-start(bf16[1,64,2048]{2,1,0:T(8,128)(2,1)} %get-tuple-element.26), channel_id=1, source_target_pairs={{0,7},{1,8},{2,9},{3,10},{4,11},{5,12},{6,13},{7,14},{8,15},{9,0},... | collective-permute-start | bytes 786440 | tf_op jit(solution)/shard_map/ppermute | solution.py:67
  679.1 38.1 %collective-permute-start.42 = (bf16[1,64,2048]{2,1,0:T(8,128)(2,1)}, bf16[1,64,2048]{2,1,0:T(8,128)(2,1)S(1)}, u32[]{:S(2)}, u32[]{:S(2)}) collective-permute-start(bf16[1,64,2048]{2,1,0:T(8,128)(2,1)} %get-tuple-element.25), channel_id=1, source_target_pairs={{0,6},{1,7},{2,8},{3,9},{4,10},{5,11},{6,12},{7,13},{8,14},{9,15},... | collective-permute-start | bytes 786440 | tf_op jit(solution)/shard_map/ppermute | solution.py:67
  697.3 37.4 %collective-permute-start.43 = (bf16[1,64,2048]{2,1,0:T(8,128)(2,1)}, bf16[1,64,2048]{2,1,0:T(8,128)(2,1)S(1)}, u32[]{:S(2)}, u32[]{:S(2)}) collective-permute-start(bf16[1,64,2048]{2,1,0:T(8,128)(2,1)} %get-tuple-element.24), channel_id=1, source_target_pairs={{0,5},{1,6},{2,7},{3,8},{4,9},{5,10},{6,11},{7,12},{8,13},{9,14},{... | collective-permute-start | bytes 786440 | tf_op jit(solution)/shard_map/ppermute | solution.py:67
  717.0 20.0 %collective-permute-start.44 = (bf16[1,64,2048]{2,1,0:T(8,128)(2,1)}, bf16[1,64,2048]{2,1,0:T(8,128)(2,1)S(1)}, u32[]{:S(2)}, u32[]{:S(2)}) collective-permute-start(bf16[1,64,2048]{2,1,0:T(8,128)(2,1)} %get-tuple-element.23), channel_id=1, source_target_pairs={{0,4},{1,5},{2,6},{3,7},{4,8},{5,9},{6,10},{7,11},{8,12},{9,13},{1... | collective-permute-start | bytes 786440 | tf_op jit(solution)/shard_map/ppermute | solution.py:67
  717.1 20.2 %collective-permute-start.45 = (bf16[1,64,2048]{2,1,0:T(8,128)(2,1)S(1)}, bf16[1,64,2048]{2,1,0:T(8,128)(2,1)S(1)}, u32[]{:S(2)}, u32[]{:S(2)}) collective-permute-start(bf16[1,64,2048]{2,1,0:T(8,128)(2,1)S(1)} %copy-done.10), channel_id=1, source_target_pairs={{0,3},{1,4},{2,5},{3,6},{4,7},{5,8},{6,9},{7,10},{8,11},{9,12},{10... | collective-permute-start | bytes 786440 | tf_op jit(solution)/shard_map/ppermute | solution.py:67
  717.2 25.7 %collective-permute-start.46 = (bf16[1,64,2048]{2,1,0:T(8,128)(2,1)S(1)}, bf16[1,64,2048]{2,1,0:T(8,128)(2,1)S(1)}, u32[]{:S(2)}, u32[]{:S(2)}) collective-permute-start(bf16[1,64,2048]{2,1,0:T(8,128)(2,1)S(1)} %copy-done.9), channel_id=1, source_target_pairs={{0,2},{1,3},{2,4},{3,5},{4,6},{5,7},{6,8},{7,9},{8,10},{9,11},{10,... | collective-permute-start | bytes 786440 | tf_op jit(solution)/shard_map/ppermute | solution.py:67
  734.7 11.5 %collective-permute-start.47 = (bf16[1,64,2048]{2,1,0:T(8,128)(2,1)S(1)}, bf16[1,64,2048]{2,1,0:T(8,128)(2,1)S(1)}, u32[]{:S(2)}, u32[]{:S(2)}) collective-permute-start(bf16[1,64,2048]{2,1,0:T(8,128)(2,1)S(1)} %copy-done.7), channel_id=1, source_target_pairs={{0,1},{1,2},{2,3},{3,4},{4,5},{5,6},{6,7},{7,8},{8,9},{9,10},{10,1... | collective-permute-start | bytes 786440 | tf_op jit(solution)/shard_map/ppermute | solution.py:67
  (17 other events, 99.2 us)
